TPU v7x, 512 devices: a whole 4x8x8 slice. The times are simulated.
512 devices in a mesh: band: 32 (over y, x), field: 16 (over z, core).
Axes of the slice: x: 4, y: 8, z: 8, core: 2. Of those that a mesh axis runs over, the one named last changes fastest.
Arguments:
- fourier: bfloat16 [144, 1024, 2, 1024], P('field', 'band'), may hold values from -6 to 6
- row_length: int32 [1024], P('band'), may hold values from 20 to 2076, as said below
- wave_order: int32 [512], replicated, may hold values from 0 to 511, each once
- legendre: bfloat16 [512, 1025, 512], P(('band', 'field')), may hold values from -0.1875 to 0.1875
- vertical: bfloat16 [2, 72, 72], replicated, may hold values from -0.75 to 0.75
Outputs:
- returned: bfloat16 [144, 1024, 2, 1024], P('field', 'band')
Inputs may be any that keep to these rules, and one draw needn't show every extreme that they name: row_length[lat] is a multiple of 4 lying 0 to 12 above 20 + 4 * d with d = min(lat, 1023 - lat); the two polar rows have length 20 and the two rows beside the equator lie 12 above. `wave_order`: each pair index appears once.
All inputs are finite; a program needn't handle non-finite values.
Results may differ from a plain program's by a relative error of at most 0.0049.
Values may be sent and summed in bfloat16 or wider, within the bound.
No kernel may reach another device: no remote copies, remote signals or barrier semaphores. Data moves between devices by JAX's collectives and lax.ppermute only.
A program may use at most 64 MiB of HBM per device.

v0:
```python
import functools

import jax
import jax.numpy as jnp
from jax import lax
from jax.experimental import pallas as pl
from jax.experimental.pallas import tpu as pltpu
from jax.sharding import PartitionSpec as P

BF16 = jnp.bfloat16
F32 = jnp.float32
ROWS = 1152
NT = (((1,), (1,)), ((), ()))
NN = (((1,), (0,)), ((), ()))


def dot(a, b, dims=NN):
    return lax.dot_general(a, b, dims, preferred_element_type=F32)


def pair_kernel(
    boundary_ref, data_ref, table_ref, mix_ref, north_ref, south_ref, out_ref,
    value_n, value_s, spectral, updated, flipped, grid_n, grid_s,
):
    halves = ((north_ref, value_n, grid_n, 0), (south_ref, value_s, grid_s, 1))

    def source(tile, half, part, width):
        rows = []
        for high in range(4):
            start = ((half * 4 + high) * 4 + part) * 32
            rows.append(data_ref[start : start + 32, tile * 128 : tile * 128 + width])
        return jnp.concatenate(rows, axis=0)

    for tile in range(5):
        width = 128 if tile < 4 else 64
        groups = width // 32
        for perm_ref, value_ref, _, half in halves:
            moved = jnp.zeros((128, groups * 128), F32)
            if width == 128:
                joined = jnp.concatenate(
                    [source(tile, half, part, width) for part in range(4)], axis=1
                )
                moved = dot(joined, perm_ref[...])
            else:
                for part in range(4):
                    moved += dot(
                        source(tile, half, part, width),
                        perm_ref[part * 128 : part * 128 + width, : groups * 128],
                    )
            moved = moved.astype(BF16)
            for high in range(4):
                place = high if half == 0 else 3 - high
                for group in range(groups):
                    row = (tile * 4 + group) * 32
                    value_ref[row : row + 32, place * 128 : place * 128 + 128] = moved[
                        high * 32 : high * 32 + 32, group * 128 : group * 128 + 128
                    ]

    boundary = boundary_ref[0]
    for start in range(0, ROWS, 256):
        size = min(256, ROWS - start)
        row_ids = lax.broadcasted_iota(jnp.int32, (1, size), 1) + start
        first = row_ids < boundary
        degree = jnp.where(first, row_ids, row_ids - boundary)
        parity = (1 - 2 * (degree & 1)).astype(F32)
        slots = lax.broadcasted_iota(jnp.int32, (576, size), 0) & 1
        owned = slots == jnp.where(first, 0, 1)
        table = table_ref[start : start + size, :]
        total = dot(value_n[...], table, NT) + parity * dot(value_s[...], table, NT)
        spectral[...] = jnp.zeros_like(spectral)
        spectral[:, :size] = jnp.where(owned, total, 0.0).astype(BF16)
        mixed = dot(mix_ref[...], spectral[:, :size])
        updated[:, start : start + size] = mixed.astype(BF16)
        flipped[:, start : start + size] = (mixed * parity).astype(BF16)

    grid_n[...] = dot(updated[...], table_ref[...]).astype(BF16)
    grid_s[...] = dot(flipped[...], table_ref[...]).astype(BF16)

    for tile in range(5):
        width = 128 if tile < 4 else 64
        groups = width // 32
        for perm_ref, _, grid_ref, half in halves:
            lanes = []
            for group in range(groups):
                row = (tile * 4 + group) * 32
                rows = []
                for high in range(4):
                    place = high if half == 0 else 3 - high
                    rows.append(grid_ref[row : row + 32, place * 128 : place * 128 + 128])
                lanes.append(jnp.concatenate(rows, axis=0))
            joined = jnp.concatenate(lanes, axis=1)
            for part in range(4):
                perm = perm_ref[part * 128 : part * 128 + width, : groups * 128]
                moved = dot(joined, perm, NT).astype(BF16)
                for high in range(4):
                    start = ((half * 4 + high) * 4 + part) * 32
                    out_ref[start : start + 32, tile * 128 : tile * 128 + width] = moved[
                        high * 32 : high * 32 + 32, :
                    ]


def transform_pair(boundary, data, table, mix, north, south):
    vmem = pl.BlockSpec(memory_space=pltpu.VMEM)
    return pl.pallas_call(
        pair_kernel,
        out_shape=jax.ShapeDtypeStruct((1024, 576), BF16),
        in_specs=[pl.BlockSpec(memory_space=pltpu.SMEM)] + [vmem] * 5,
        out_specs=vmem,
        scratch_shapes=[
            pltpu.VMEM((576, 512), BF16),
            pltpu.VMEM((576, 512), BF16),
            pltpu.VMEM((576, 256), BF16),
            pltpu.VMEM((576, ROWS), BF16),
            pltpu.VMEM((576, ROWS), BF16),
            pltpu.VMEM((576, 512), BF16),
            pltpu.VMEM((576, 512), BF16),
        ],
        compiler_params=pltpu.CompilerParams(vmem_limit_bytes=40 * 1024 * 1024),
        cost_estimate=pl.CostEstimate(
            flops=5_000_000_000, bytes_accessed=6_000_000, transcendentals=0
        ),
    )(boundary, data, table, mix, north, south)


def lane_moves():
    row = lax.broadcasted_iota(jnp.int32, (512, 512), 0)
    column = lax.broadcasted_iota(jnp.int32, (512, 512), 1)
    part, f, lat, c = row >> 7, (row >> 6) & 1, (row >> 1) & 31, row & 1
    place = part * 32 + lat
    start = f * 256 + c * 128
    north = (column == start + place).astype(BF16)
    south = (column == start + 127 - place).astype(BF16)
    return north, south


def mixing_matrix(vertical):
    row = lax.broadcasted_iota(jnp.int32, (576, 144), 0)
    level = lax.broadcasted_iota(jnp.int32, (576, 144), 1)
    pick = (level == 9 * ((row >> 1) & 15) + (row >> 6)).astype(BF16)
    nothing = jnp.zeros_like(vertical[0])
    whole = jnp.concatenate(
        [
            jnp.concatenate([vertical[0], nothing], axis=1),
            jnp.concatenate([nothing, vertical[1]], axis=1),
        ],
        axis=0,
    )
    spread = dot(dot(pick, whole).astype(BF16), pick, NT).astype(BF16)
    r = lax.broadcasted_iota(jnp.int32, (576, 576), 0)
    q = lax.broadcasted_iota(jnp.int32, (576, 576), 1)
    same = (r & 33) == (q & 33)
    return jnp.where(same, spread, jnp.zeros((), BF16))


def per_device(fourier, row_length, wave_order, legendre, vertical):
    field_count = lax.axis_size("field")
    position = lax.axis_index("band") * field_count + lax.axis_index("field")
    wave_ids = lax.iota(jnp.int32, 1024)
    in_range = wave_ids[None, :] < jnp.minimum(1024, row_length // 2)[:, None]
    in_range = in_range[None, :, None, :]
    nothing = jnp.zeros((), BF16)
    ordering = jnp.stack([wave_order, 1023 - wave_order], axis=1).reshape(1024, 1)
    chosen = (ordering == wave_ids[None, :]).astype(BF16)
    masked = jnp.where(in_range, fourier, nothing).reshape(576, 1024)
    outgoing = lax.dot_general(chosen, masked, NT, preferred_element_type=BF16)
    arrived = lax.all_to_all(
        outgoing.reshape(512, 2, 576), ("band", "field"), split_axis=0, concat_axis=0, tiled=True
    ).reshape(1024, 576)
    boundary = 1024 - lax.dynamic_slice_in_dim(wave_order, position, 1)
    table = jnp.pad(legendre[0], ((0, ROWS - 1025), (0, 0)))
    north, south = lane_moves()
    mix = mixing_matrix(vertical)
    result = transform_pair(boundary, arrived, table, mix, north, south)
    back = lax.all_to_all(
        result.reshape(512, 2, 576), ("band", "field"), split_axis=0, concat_axis=0, tiled=True
    ).reshape(1024, 576)
    restored = lax.dot_general(
        back, chosen, (((0,), (0,)), ((), ())), preferred_element_type=BF16
    ).reshape(9, 32, 2, 1024)
    return jnp.where(in_range, restored, nothing)


def solution(mesh):
    placed = (P("field", "band", None, None), P("band"), P(), P(("band", "field"), None, None), P())
    return jax.shard_map(
        per_device,
        mesh=mesh,
        in_specs=placed,
        out_specs=P("field", "band", None, None),
        check_vma=False,
    )
```

profile of v0, /device:TPU:1, one launch (start us, length us, event | category | flops | bytes accessed | tf_op | source)
XLA Modules:
  0.0 137.3 jit_solution(5563094813326122368)
XLA Ops:
  0.0 0.7 fusion.42
  0.7 0.7 broadcast_subtract_fusion
  1.3 0.1 iota_compare_fusion.9
  1.4 1.5 %copy_select_fusion = bf16[9,32,2,1024]{3,1,2,0:T(8,128)(2,1)S(1)} fusion(bf16[9,32,2,1024]{3,2,1,0:T(2,128)(2,1)} %param.5, pred[32,1024]{1,0:T(8,128)(4,1)S(1)} %iota_compare_fusion.9), kind=kLoop, calls=%fused_computation.12 | loop fusion | flops 589824 | bytes 2392064 | tf_op jit(solution)/shard_map/jit(_where)/select_n | solution.py:164
  2.9 1.2 copy.24
  4.2 0.0 copy-start.5
  4.2 0.5 reshape.60
  4.7 0.2 copy-done.5
  4.9 1.6 %fusion.1 = bf16[512,2,576]{0,2,1:T(8,128)(2,1)S(1)} fusion(bf16[576,1024,1]{1,0,2:T(8,128)(2,1)S(1)} %reshape.60, s32[512,2]{0,1:T(2,128)S(1)} %pad_add_fusion), kind=kOutput, calls=%fused_computation.3 | convolution fusion | flops 1209008128 | bytes 2363392 | tf_op jit(solution)/shard_map/dot_general | solution.py:165
  6.5 2.8 %copy.25 = bf16[512,2,576]{2,1,0:T(2,128)(2,1)} copy(bf16[512,2,576]{0,2,1:T(8,128)(2,1)S(1)} %fusion.1) | data formatting | bytes 2359296 | tf_op jit(solution)/shard_map/dot_general | solution.py:165
  9.3 22.2 %all-to-all-start = ((bf16[512,2,576]{2,1,0:T(2,128)(2,1)}), bf16[512,2,576]{2,1,0:T(2,128)(2,1)S(1)}, u32[]{:S(2)}, u32[]{:S(2)}) async-start(bf16[512,2,576]{2,1,0:T(2,128)(2,1)} %copy.25), calls=%async_computation | async-start | bytes 2621440 | tf_op jit(solution)/shard_map/all_to_all | solution.py:166
  31.5 0.0 copy-start.4
  31.5 0.6 dynamic_slice.3
  32.7 1.1 pad.6.table_ref
  33.9 1.7 %compare_select_fusion.mix_ref = bf16[576,576]{1,0:T(8,128)(2,1)} fusion(s32[576]{0:T(1024)S(1)} %get-tuple-element.8, s32[576]{0:T(1024)S(1)} %get-tuple-element.7, bf16[72,72]{1,0:T(8,128)(2,1)S(1)} %get-tuple-element.6, bf16[72,72]{1,0:T(8,128)(2,1)S(1)} %get-tuple-element.5), kind=kOutput, calls=%fused_computation.8 | convolution fusion | flops 120849408 | bytes 688896 | tf_op jit(solution)/shard_map/dot_general | solution.py:18
  35.6 1.0 fusion.12
  36.6 33.9 %all-to-all-done = bf16[512,2,576]{2,1,0:T(2,128)(2,1)S(1)} async-done(((bf16[512,2,576]{2,1,0:T(2,128)(2,1)}), bf16[512,2,576]{2,1,0:T(2,128)(2,1)S(1)}, u32[]{:S(2)}, u32[]{:S(2)}) %all-to-all-start) | async-done | bytes 1179680 | tf_op jit(solution)/shard_map/all_to_all | solution.py:166
  70.5 1.0 reshape.57.data_ref
  71.6 1.3 copy-done
  72.8 1.0 copy-done.1
  73.9 1.1 copy-done.2
  75.0 7.4 %shard_map.55 = bf16[1024,576]{1,0:T(8,128)(2,1)S(1)} custom-call(s32[1]{0:T(128)S(6)} %sub.20.boundary_ref, bf16[1024,576]{1,0:T(8,128)(2,1)S(1)} %reshape.57.data_ref, bf16[1152,512]{1,0:T(8,128)(2,1)S(1)} %copy-done, bf16[576,576]{1,0:T(8,128)(2,1)S(1)} %copy-done.2, bf16[512,512]{1,0:T(8,128)(2,1)S(1)} %get-tuple-element.9.north_ref, ...), custom_call_target="tpu_custom_call" | custom-call | flops 5000000000 | bytes 6000000 | tf_op jit(solution)/shard_map/pallas_call | solution.py:104
  82.4 1.4 %reshape.58 = bf16[512,2,576]{2,1,0:T(2,128)(2,1)} reshape(bf16[1024,576]{1,0:T(8,128)(2,1)S(1)} %shard_map.55) | data formatting | bytes 2359296 | tf_op jit(solution)/shard_map/reshape | solution.py:175
  83.9 8.6 %all-to-all-start.1 = ((bf16[512,2,576]{2,1,0:T(2,128)(2,1)}), bf16[512,2,576]{2,1,0:T(2,128)(2,1)S(1)}, u32[]{:S(2)}, u32[]{:S(2)}) async-start(bf16[512,2,576]{2,1,0:T(2,128)(2,1)} %reshape.58), calls=%async_computation.1 | async-start | bytes 2621440 | tf_op jit(solution)/shard_map/all_to_all | solution.py:174
  92.4 0.1 copy.27
  92.6 0.2 eq.59
  92.8 38.5 %all-to-all-done.1 = bf16[512,2,576]{2,1,0:T(2,128)(2,1)S(1)} async-done(((bf16[512,2,576]{2,1,0:T(2,128)(2,1)}), bf16[512,2,576]{2,1,0:T(2,128)(2,1)S(1)}, u32[]{:S(2)}, u32[]{:S(2)}) %all-to-all-start.1) | async-done | bytes 1179680 | tf_op jit(solution)/shard_map/all_to_all | solution.py:174
  131.3 1.0 reshape.59
  132.4 0.6 copy.26
  133.0 0.5 dot_general.20
  133.5 1.6 %fusion.8 = bf16[9,32,2,1024]{3,1,2,0:T(8,128)(2,1)S(1)} fusion(s32[1024]{0:T(1024)S(1)} %eq.59, bf16[9,32,2,1024]{3,2,1,0:T(2,128)(2,1)S(1)} %dot_general.20, pred[32,1024]{1,0:T(8,128)(4,1)S(1)} %iota_compare_fusion.9), kind=kOutput, calls=%fused_computation.10 | convolution fusion | flops 1209597952 | bytes 2396160 | tf_op jit(solution)/shard_map/dot_general | solution.py:177
  135.0 2.2 %copy.29 = bf16[9,32,2,1024]{3,2,1,0:T(2,128)(2,1)} copy(bf16[9,32,2,1024]{3,1,2,0:T(8,128)(2,1)S(1)} %fusion.8) | data formatting | bytes 2359296 | tf_op jit(solution)/shard_map/jit(_where)/select_n | solution.py:180
  (11 shorter events, 0.0 us)
Async XLA Ops:
  4.2 0.7 copy-start.5
  9.3 23.4 %copy-start.3 = (bf16[1,1025,512]{2,1,0:T(8,128)(2,1)S(1)}, bf16[1,1025,512]{2,1,0:T(8,128)(2,1)}, u32[]{:S(2)}) copy-start(bf16[1,1025,512]{2,1,0:T(8,128)(2,1)} %param.8) | copy-start | bytes 3148804
  9.3 61.2 %all-to-all-start = ((bf16[512,2,576]{2,1,0:T(2,128)(2,1)}), bf16[512,2,576]{2,1,0:T(2,128)(2,1)S(1)}, u32[]{:S(2)}, u32[]{:S(2)}) async-start(bf16[512,2,576]{2,1,0:T(2,128)(2,1)} %copy.25), calls=%async_computation | async-start | bytes 2621440 | tf_op jit(solution)/shard_map/all_to_all | solution.py:166
  31.5 2.4 %copy-start.4 = (bf16[2,72,72]{2,1,0:T(8,128)(2,1)S(1)}, bf16[2,72,72]{2,1,0:T(8,128)(2,1)}, u32[]{:S(2)}) copy-start(bf16[2,72,72]{2,1,0:T(8,128)(2,1)} %param.9) | copy-start | bytes 62212
  71.6 1.3 copy-start
  72.8 1.0 copy-start.1
  73.9 1.1 copy-start.2
  83.9 47.4 %all-to-all-start.1 = ((bf16[512,2,576]{2,1,0:T(2,128)(2,1)}), bf16[512,2,576]{2,1,0:T(2,128)(2,1)S(1)}, u32[]{:S(2)}, u32[]{:S(2)}) async-start(bf16[512,2,576]{2,1,0:T(2,128)(2,1)} %reshape.58), calls=%async_computation.1 | async-start | bytes 2621440 | tf_op jit(solution)/shard_map/all_to_all | solution.py:174
where the time goes:
time: 138 us; the launch traced here: 137 us
  waiting for transfers between devices  72.4 us (52%)
  starting transfers between devices  30.7 us (22%)
  local copies, waits for them, and re-layouts  17 us (12%)
  Pallas kernels  7.42 us (5%)
  matrix products  4.87 us (4%)
  other arithmetic  3.99 us (3%)
    all_to_all x1, waiting for transfers between devices, per_device(): lax.all_to_all(result.reshape(512, 2, 576), ('band', 'field'), split_axis...  38.5 us
    all_to_all x1, waiting for transfers between devices, per_device(): lax.all_to_all(outgoing.reshape(512, 2, 576), ('band', 'field'), split_ax...  33.9 us
    all_to_all x1, starting transfers between devices, per_device(): lax.all_to_all(outgoing.reshape(512, 2, 576), ('band', 'field'), split_ax...  22.2 us
    all_to_all x1, starting transfers between devices, per_device(): lax.all_to_all(result.reshape(512, 2, 576), ('band', 'field'), split_axis...  8.57 us
    pallas_call x1, Pallas kernels, transform_pair(): pl.pallas_call(pair_kernel, out_shape=jax.ShapeDtypeStruct((1024, 576), B...  7.42 us
    unnamed x12, local copies, waits for them, and re-layouts  3.61 us
    dot_general x1, local copies, waits for them, and re-layouts, per_device(): outgoing = lax.dot_general(chosen, masked, NT, preferred_element_type=BF16)  2.83 us
  transfers between devices with their start and end apart: 2, of which 2 were waited for; matrix products, arithmetic and copies ran while one was open for 3% of the time, Pallas kernels for 0%

commit v1 on v0

--- a/solution.py
+++ b/solution.py
@@ -19,16 +19,33 @@
 
 
 def pair_kernel(
-    boundary_ref, data_ref, table_ref, mix_ref, north_ref, south_ref, out_ref,
-    value_n, value_s, spectral, updated, flipped, grid_n, grid_s,
+    boundary_ref, data_ref, north_hbm, south_hbm, table_hbm, mix_hbm, out_ref,
+    north_ref, south_ref, table_ref, mix_ref,
+    value_n, value_s, spectral, updated, flipped, grid_n, grid_s, sems,
 ):
+    copies = [
+        pltpu.make_async_copy(source, target, sems.at[i])
+        for i, (source, target) in enumerate(
+            (
+                (north_hbm, north_ref),
+                (south_hbm, south_ref),
+                (table_hbm, table_ref),
+                (mix_hbm, mix_ref),
+            )
+        )
+    ]
+    for copy in copies:
+        copy.start()
+    copies[0].wait()
+    copies[1].wait()
     halves = ((north_ref, value_n, grid_n, 0), (south_ref, value_s, grid_s, 1))
 
     def source(tile, half, part, width):
         rows = []
         for high in range(4):
-            start = ((half * 4 + high) * 4 + part) * 32
-            rows.append(data_ref[start : start + 32, tile * 128 : tile * 128 + width])
+            start = ((half * 4 + high) * 4 + part) * 16
+            block = data_ref[start : start + 16, :, tile * 128 : tile * 128 + width]
+            rows.append(block.reshape(32, width))
         return jnp.concatenate(rows, axis=0)
 
     for tile in range(5):
@@ -56,6 +73,8 @@
                         high * 32 : high * 32 + 32, group * 128 : group * 128 + 128
                     ]
 
+    copies[2].wait()
+    copies[3].wait()
     boundary = boundary_ref[0]
     for start in range(0, ROWS, 256):
         size = min(256, ROWS - start)
@@ -93,20 +112,22 @@
                 perm = perm_ref[part * 128 : part * 128 + width, : groups * 128]
                 moved = dot(joined, perm, NT).astype(BF16)
                 for high in range(4):
-                    start = ((half * 4 + high) * 4 + part) * 32
-                    out_ref[start : start + 32, tile * 128 : tile * 128 + width] = moved[
-                        high * 32 : high * 32 + 32, :
-                    ]
-
-
-def transform_pair(boundary, data, table, mix, north, south):
-    vmem = pl.BlockSpec(memory_space=pltpu.VMEM)
+                    start = ((half * 4 + high) * 4 + part) * 16
+                    block = moved[high * 32 : high * 32 + 32, :].reshape(16, 2, width)
+                    out_ref[start : start + 16, :, tile * 128 : tile * 128 + width] = block
+
+
+def transform_pair(boundary, data, north, south, table, mix):
     return pl.pallas_call(
         pair_kernel,
-        out_shape=jax.ShapeDtypeStruct((1024, 576), BF16),
-        in_specs=[pl.BlockSpec(memory_space=pltpu.SMEM)] + [vmem] * 5,
-        out_specs=vmem,
+        out_shape=jax.ShapeDtypeStruct((512, 2, 576), BF16),
+        in_specs=[pl.BlockSpec(memory_space=pltpu.SMEM), VMEM, HBM, HBM, HBM, HBM],
+        out_specs=VMEM,
         scratch_shapes=[
+            pltpu.VMEM((512, 512), BF16),
+            pltpu.VMEM((512, 512), BF16),
+            pltpu.VMEM((ROWS, 512), BF16),
+            pltpu.VMEM((576, 576), BF16),
             pltpu.VMEM((576, 512), BF16),
             pltpu.VMEM((576, 512), BF16),
             pltpu.VMEM((576, 256), BF16),
@@ -114,12 +135,13 @@
             pltpu.VMEM((576, ROWS), BF16),
             pltpu.VMEM((576, 512), BF16),
             pltpu.VMEM((576, 512), BF16),
+            pltpu.SemaphoreType.DMA((4,)),
         ],
-        compiler_params=pltpu.CompilerParams(vmem_limit_bytes=40 * 1024 * 1024),
+        compiler_params=pltpu.CompilerParams(vmem_limit_bytes=16 * 1024 * 1024),
         cost_estimate=pl.CostEstimate(
             flops=5_000_000_000, bytes_accessed=6_000_000, transcendentals=0
         ),
-    )(boundary, data, table, mix, north, south)
+    )(boundary, data, *(pltpu.with_memory_space_constraint(x, pltpu.HBM) for x in (north, south, table, mix)))
 
 
 def lane_moves():
@@ -152,32 +174,136 @@
     return jnp.where(same, spread, jnp.zeros((), BF16))
 
 
+def column_of(values, rows):
+    count = values.shape[1]
+    row = lax.broadcasted_iota(jnp.int32, (16, count), 0)
+    digits = jnp.where(row == 0, values >> 5, jnp.where(row == 1, values & 31, 0))
+    row = lax.broadcasted_iota(jnp.int32, (rows, count), 0)
+    lane = lax.broadcasted_iota(jnp.int32, (rows, count), 1)
+    repeat = jnp.where((row >> 1) == lane, 1.0, 0.0).astype(BF16)
+    columns = dot(repeat, digits.astype(F32).astype(BF16), NT)
+    return columns[:, 0:1] * 32.0 + columns[:, 1:2]
+
+
+def wave_mask(row_length_ref):
+    count = jnp.minimum(1024, row_length_ref[...] >> 1)
+    limit = column_of(count, 64).astype(jnp.int32)
+    return lax.broadcasted_iota(jnp.int32, (64, 1024), 1) < limit
+
+
+def order_kernel(
+    length_hbm, order_hbm, fourier_hbm, out_hbm, chosen_ref,
+    lengths, order, raw, masked, out, in_sems, out_sems,
+):
+    copies = [
+        pltpu.make_async_copy(source, target, in_sems.at[i])
+        for i, (source, target) in enumerate(
+            ((order_hbm, order), (length_hbm, lengths), (fourier_hbm, raw))
+        )
+    ]
+    for copy in copies:
+        copy.start()
+    wave_ids = lax.broadcasted_iota(jnp.int32, (256, 1024), 1)
+    odd = (lax.broadcasted_iota(jnp.int32, (256, 1), 0) & 1) == 1
+    copies[0].wait()
+    for block in range(4):
+        wave = column_of(order[:, block * 128 : block * 128 + 128], 256).astype(jnp.int32)
+        wave = jnp.where(odd, 1023 - wave, wave)
+        picked = jnp.where(wave_ids == wave, 1.0, 0.0).astype(BF16)
+        chosen_ref[block * 256 : block * 256 + 256, :] = picked
+    copies[1].wait()
+    in_range = wave_mask(lengths)
+    copies[2].wait()
+    for f in range(9):
+        kept = jnp.where(in_range, raw[f].reshape(64, 1024), jnp.zeros((), BF16))
+        masked[f * 64 : f * 64 + 64, :] = kept
+    sent = []
+    for block in range(4):
+        sorted_rows = dot(chosen_ref[block * 256 : block * 256 + 256, :], masked[...], NT)
+        part = slice(block * 128, block * 128 + 128)
+        out[part] = sorted_rows.astype(BF16).reshape(128, 2, 576)
+        copy = pltpu.make_async_copy(out.at[part], out_hbm.at[part], out_sems.at[block])
+        copy.start()
+        sent.append(copy)
+    for copy in sent:
+        copy.wait()
+
+
+def restore_kernel(length_ref, chosen_ref, data_ref, out_hbm, turned, out, sems):
+    in_range = wave_mask(length_ref)
+    for block in range(8):
+        rows = data_ref[block * 64 : block * 64 + 64].reshape(128, 576)
+        turned[:, block * 128 : block * 128 + 128] = rows.T
+    sent = []
+    for start, size in ((0, 4), (4, 4), (8, 1)):
+        restored = dot(turned[start * 64 : (start + size) * 64, :], chosen_ref[...])
+        for f in range(size):
+            kept = jnp.where(in_range, restored[f * 64 : f * 64 + 64, :], 0.0).astype(BF16)
+            out[start + f] = kept.reshape(32, 2, 1024)
+        part = slice(start, start + size)
+        copy = pltpu.make_async_copy(out.at[part], out_hbm.at[part], sems.at[len(sent)])
+        copy.start()
+        sent.append(copy)
+    for copy in sent:
+        copy.wait()
+
+
+VMEM = pl.BlockSpec(memory_space=pltpu.VMEM)
+HBM = pl.BlockSpec(memory_space=pltpu.HBM)
+
+
+def order_pairs(row_length, wave_order, fourier):
+    return pl.pallas_call(
+        order_kernel,
+        out_shape=(
+            pltpu.HBM((512, 2, 576), BF16),
+            pltpu.VMEM((1024, 1024), BF16),
+        ),
+        in_specs=[HBM, HBM, HBM],
+        out_specs=(HBM, VMEM),
+        scratch_shapes=[
+            pltpu.VMEM((1, 32), jnp.int32),
+            pltpu.VMEM((1, 512), jnp.int32),
+            pltpu.VMEM((9, 32, 2, 1024), BF16),
+            pltpu.VMEM((576, 1024), BF16),
+            pltpu.VMEM((512, 2, 576), BF16),
+            pltpu.SemaphoreType.DMA((3,)),
+            pltpu.SemaphoreType.DMA((4,)),
+        ],
+        compiler_params=pltpu.CompilerParams(vmem_limit_bytes=16 * 1024 * 1024),
+    )(*(pltpu.with_memory_space_constraint(x, pltpu.HBM) for x in (row_length, wave_order, fourier)))
+
+
+def restore_waves(row_length, chosen, data):
+    return pl.pallas_call(
+        restore_kernel,
+        out_shape=jax.ShapeDtypeStruct((9, 32, 2, 1024), BF16),
+        in_specs=[VMEM, VMEM, VMEM],
+        out_specs=HBM,
+        scratch_shapes=[
+            pltpu.VMEM((576, 1024), BF16),
+            pltpu.VMEM((9, 32, 2, 1024), BF16),
+            pltpu.SemaphoreType.DMA((3,)),
+        ],
+        compiler_params=pltpu.CompilerParams(vmem_limit_bytes=16 * 1024 * 1024),
+    )(row_length, chosen, data)
+
+
+def exchange(chunks):
+    return lax.all_to_all(chunks, ("band", "field"), split_axis=0, concat_axis=0, tiled=True)
+
+
 def per_device(fourier, row_length, wave_order, legendre, vertical):
-    field_count = lax.axis_size("field")
-    position = lax.axis_index("band") * field_count + lax.axis_index("field")
-    wave_ids = lax.iota(jnp.int32, 1024)
-    in_range = wave_ids[None, :] < jnp.minimum(1024, row_length // 2)[:, None]
-    in_range = in_range[None, :, None, :]
-    nothing = jnp.zeros((), BF16)
-    ordering = jnp.stack([wave_order, 1023 - wave_order], axis=1).reshape(1024, 1)
-    chosen = (ordering == wave_ids[None, :]).astype(BF16)
-    masked = jnp.where(in_range, fourier, nothing).reshape(576, 1024)
-    outgoing = lax.dot_general(chosen, masked, NT, preferred_element_type=BF16)
-    arrived = lax.all_to_all(
-        outgoing.reshape(512, 2, 576), ("band", "field"), split_axis=0, concat_axis=0, tiled=True
-    ).reshape(1024, 576)
+    position = lax.axis_index("band") * lax.axis_size("field") + lax.axis_index("field")
+    lengths = row_length.reshape(1, 32)
+    outgoing, chosen = order_pairs(lengths, wave_order.reshape(1, 512), fourier)
+    arrived = exchange(outgoing)
     boundary = 1024 - lax.dynamic_slice_in_dim(wave_order, position, 1)
     table = jnp.pad(legendre[0], ((0, ROWS - 1025), (0, 0)))
     north, south = lane_moves()
     mix = mixing_matrix(vertical)
-    result = transform_pair(boundary, arrived, table, mix, north, south)
-    back = lax.all_to_all(
-        result.reshape(512, 2, 576), ("band", "field"), split_axis=0, concat_axis=0, tiled=True
-    ).reshape(1024, 576)
-    restored = lax.dot_general(
-        back, chosen, (((0,), (0,)), ((), ())), preferred_element_type=BF16
-    ).reshape(9, 32, 2, 1024)
-    return jnp.where(in_range, restored, nothing)
+    result = transform_pair(boundary, arrived, north, south, table, mix)
+    return restore_waves(lengths, chosen, exchange(result))
 
 
 def solution(mesh):

time: 138 us -> 125 us (0.906)
  blocking collectives: 0 us -> 47.3 us
  waiting for transfers between devices: 72.4 us -> 32 us
  local copies, waits for them, and re-layouts: 17 us -> 3.6 us
  Pallas kernels: 7.42 us -> 16.3 us
  starting transfers between devices: 30.7 us -> 22.2 us
  matrix products: 4.87 us -> 1.49 us
  other arithmetic: 3.99 us -> 1.26 us
    all_to_all x0 -> x1, blocking collectives: none -> 47.3 us  [exchange(): lax.all_to_all(chunks, ('band', 'field'), split_axis=0, concat_axis=0, ti...]
    all_to_all x2 -> x1, waiting for transfers between devices: 72.4 us -> 32 us  [exchange(): lax.all_to_all(chunks, ('band', 'field'), split_axis=0, concat_axis=0, ti...]
    pallas_call x1 -> x3, Pallas kernels: 7.42 us -> 16.3 us  [the longest x1 9.11 us: transform_pair(): pl.pallas_call(pair_kernel, out_shape=jax.ShapeDtypeStruct((512, 2, 576),...]
    all_to_all x2 -> x1, starting transfers between devices: 30.7 us -> 22.2 us  [exchange(): lax.all_to_all(chunks, ('band', 'field'), split_axis=0, concat_axis=0, ti...]
    reshape x4 -> x0, local copies, waits for them, and re-layouts: 4.01 us -> none  [the longest x1 1.43 us: per_device(): result.reshape(512, 2, 576)]
    dot_general x3 -> x0, local copies, waits for them, and re-layouts: 3.94 us -> none  [the longest x1 2.83 us: per_device(): outgoing = lax.dot_general(chosen, masked, NT, preferred_element_type=BF16)]
    unnamed x12 -> x4, local copies, waits for them, and re-layouts: 3.61 us -> 0.01 us
    select_n x2 -> x0, local copies, waits for them, and re-layouts: 3.45 us -> none  [the longest x1 2.23 us: per_device(): return jnp.where(in_range, restored, nothing)]
  transfers between devices with their start and end apart: 2 -> 1, of which waited for: 2 -> 1; matrix products, arithmetic and copies ran while one was open for 3% -> 5% of each run, Pallas kernels for 0% -> 0%
where the time goes in v1:
time: 125 us
  blocking collectives  47.3 us (38%)
  waiting for transfers between devices  32 us (26%)
  starting transfers between devices  22.2 us (18%)
  Pallas kernels  16.3 us (13%)
  local copies, waits for them, and re-layouts  3.6 us (3%)
  matrix products  1.49 us (1%)
  other arithmetic  1.26 us (1%)
    all_to_all x1, blocking collectives, exchange(): lax.all_to_all(chunks, ('band', 'field'), split_axis=0, concat_axis=0, ti...  47.3 us
    all_to_all x1, waiting for transfers between devices, exchange(): lax.all_to_all(chunks, ('band', 'field'), split_axis=0, concat_axis=0, ti...  32 us
    all_to_all x1, starting transfers between devices, exchange(): lax.all_to_all(chunks, ('band', 'field'), split_axis=0, concat_axis=0, ti...  22.2 us
    pallas_call x1, Pallas kernels, transform_pair(): pl.pallas_call(pair_kernel, out_shape=jax.ShapeDtypeStruct((512, 2, 576),...  9.11 us
    pallas_call x1, Pallas kernels, order_pairs(): pl.pallas_call(order_kernel, out_shape=(pltpu.HBM((512, 2, 576), BF16), p...  4.62 us
    pallas_call x1, Pallas kernels, restore_waves(): pl.pallas_call(restore_kernel, out_shape=jax.ShapeDtypeStruct((9, 32, 2,...  2.55 us
  transfers between devices with their start and end apart: 1, of which 1 were waited for; matrix products, arithmetic and copies ran while one was open for 5% of the time, Pallas kernels for 0%

profile of v1, /device:TPU:1, one launch (start us, length us, event | category | flops | bytes accessed | tf_op | source)
XLA Modules:
  0.0 125.0 jit_solution(15340401285064851158)
XLA Ops:
  0.0 4.6 %shard_map.55 = (bf16[512,2,576]{2,1,0:T(2,128)(2,1)}, bf16[1024,1024]{1,0:T(8,128)(2,1)S(1)}) custom-call(s32[1,32]{1,0:T(1,128)} %bitcast.7, s32[1,512]{1,0:T(1,128)} %bitcast.10, bf16[9,32,2,1024]{3,2,1,0:T(2,128)(2,1)} %fourier_hbm.1), custom_call_target="tpu_custom_call" | custom-call | tf_op jit(solution)/shard_map/pallas_call | solution.py:256
  4.6 22.2 %all-to-all-start = ((bf16[512,2,576]{2,1,0:T(2,128)(2,1)}), bf16[512,2,576]{2,1,0:T(2,128)(2,1)S(1)}, u32[]{:S(2)}, u32[]{:S(2)}) async-start(bf16[512,2,576]{2,1,0:T(2,128)(2,1)} %get-tuple-element.8), calls=%async_computation | async-start | bytes 2621440 | tf_op jit(solution)/shard_map/all_to_all | solution.py:293
  26.8 0.0 copy-start.1
  26.8 1.3 %dynamic_slice.3 = s32[1]{0:T(128)} dynamic-slice(s32[512]{0:T(512)} %param.7, s32[]{:T(128)S(6)} %select_n.7), dynamic_slice_sizes={1} | dynamic-slice | bytes 12 | tf_op jit(solution)/shard_map/dynamic_slice | solution.py:301
  28.8 2.3 %pad.6.table_hbm = bf16[1152,512]{1,0:T(8,128)(2,1)} pad(bf16[1025,512]{1,0:T(8,128)(2,1)} %bitcast.9, bf16[]{:T(256)} %constant.16.clone.1), padding=0_127x0_0 | pad | bytes 2229250 | tf_op jit(solution)/shard_map/jit(_pad)/pad | solution.py:302
  31.1 0.0 copy-done.1
  31.1 1.5 %compare_select_fusion.mix_hbm = bf16[576,576]{1,0:T(8,128)(2,1)} fusion(s32[576]{0:T(1024)S(1)} %get-tuple-element.12, s32[576]{0:T(1024)S(1)} %get-tuple-element.11, bf16[72,72]{1,0:T(8,128)(2,1)S(1)} %get-tuple-element.10, bf16[72,72]{1,0:T(8,128)(2,1)S(1)} %get-tuple-element.9), kind=kOutput, calls=%fused_computation | convolution fusion | flops 120849408 | bytes 688896 | tf_op jit(solution)/shard_map/dot_general | solution.py:18
  32.6 1.2 fusion
  33.8 32.0 %all-to-all-done.data_ref = bf16[512,2,576]{2,1,0:T(2,128)(2,1)S(1)} async-done(((bf16[512,2,576]{2,1,0:T(2,128)(2,1)}), bf16[512,2,576]{2,1,0:T(2,128)(2,1)S(1)}, u32[]{:S(2)}, u32[]{:S(2)}) %all-to-all-start) | async-done | bytes 1179680 | tf_op jit(solution)/shard_map/all_to_all | solution.py:293
  65.9 9.1 %shard_map.56 = bf16[512,2,576]{2,1,0:T(2,128)(2,1)S(1)} custom-call(s32[1]{0:T(128)S(6)} %sub.7.boundary_ref, bf16[512,2,576]{2,1,0:T(2,128)(2,1)S(1)} %all-to-all-done.data_ref, bf16[512,512]{1,0:T(8,128)(2,1)} %get-tuple-element.13.north_hbm, bf16[512,512]{1,0:T(8,128)(2,1)} %get-tuple-element.14.south_hbm, bf16[1152,512]{1,0:T(8,128)(2,1)} %pad.6.table_hbm, ...), custom_call_target="tpu_custom_call" | custom-call | flops 5000000000 | bytes 6000000 | tf_op jit(solution)/shard_map/pallas_call | solution.py:121
  75.0 0.0 copy-start
  75.0 47.3 %all_to_all.10.data_ref = bf16[512,2,576]{2,1,0:T(2,128)(2,1)S(1)} all-to-all(bf16[512,2,576]{2,1,0:T(2,128)(2,1)S(1)} %shard_map.56), channel_id=1, replica_groups=mesh['band'=32,'field'=16] {'band','field'}, dimensions={0} | all-to-all | bytes 2359296 | tf_op jit(solution)/shard_map/all_to_all | solution.py:293
  122.3 0.0 copy-done
  122.3 2.5 %shard_map.57 = bf16[9,32,2,1024]{3,2,1,0:T(2,128)(2,1)} custom-call(s32[1,32]{1,0:T(1,128)S(1)} %bitcast.8, bf16[1024,1024]{1,0:T(8,128)(2,1)S(1)} %get-tuple-element.7.chosen_ref, bf16[512,2,576]{2,1,0:T(2,128)(2,1)S(1)} %all_to_all.10.data_ref), custom_call_target="tpu_custom_call" | custom-call | tf_op jit(solution)/shard_map/pallas_call | solution.py:278
  (4 shorter events, 0.0 us)
Async XLA Ops:
  4.6 61.2 %all-to-all-start = ((bf16[512,2,576]{2,1,0:T(2,128)(2,1)}), bf16[512,2,576]{2,1,0:T(2,128)(2,1)S(1)}, u32[]{:S(2)}, u32[]{:S(2)}) async-start(bf16[512,2,576]{2,1,0:T(2,128)(2,1)} %get-tuple-element.8), calls=%async_computation | async-start | bytes 2621440 | tf_op jit(solution)/shard_map/all_to_all | solution.py:293
  26.8 4.3 %copy-start.1 = (bf16[2,72,72]{2,1,0:T(8,128)(2,1)S(1)}, bf16[2,72,72]{2,1,0:T(8,128)(2,1)}, u32[]{:S(2)}) copy-start(bf16[2,72,72]{2,1,0:T(8,128)(2,1)} %param.9) | copy-start | bytes 62212
  75.0 47.3 %copy-start = (s32[32]{0:T(128)S(1)}, s32[32]{0:T(128)}, u32[]{:S(2)}) copy-start(s32[32]{0:T(128)} %param.6) | copy-start | bytes 388

commit v2 on v1

v2 whole, which is shorter than its diff:
```python
import functools

import jax
import jax.numpy as jnp
from jax import lax
from jax.experimental import pallas as pl
from jax.experimental.pallas import tpu as pltpu
from jax.sharding import PartitionSpec as P

BF16 = jnp.bfloat16
F32 = jnp.float32
ROWS = 1152
EVEN = 640
NT = (((1,), (1,)), ((), ()))
NN = (((1,), (0,)), ((), ()))


def dot(a, b, dims=NN):
    return lax.dot_general(a, b, dims, preferred_element_type=F32)


def prepare_kernel(
    boundary_ref, legendre_ref, vertical_ref,
    north_ref, south_ref, north_back, south_back, table_ref, table_t, mix_ref, padded,
):
    row = lax.broadcasted_iota(jnp.int32, (512, 512), 0)
    column = lax.broadcasted_iota(jnp.int32, (512, 512), 1)
    for a, b, north, south in ((row, column, north_ref, south_ref), (column, row, north_back, south_back)):
        place = (a >> 7) * 32 + ((a >> 1) & 31)
        start = ((a >> 6) & 1) * 256 + (a & 1) * 128
        north[...] = jnp.where(b == start + place, 1.0, 0.0).astype(BF16)
        south[...] = jnp.where(b == start + 127 - place, 1.0, 0.0).astype(BF16)
    padded[:1024, :] = legendre_ref[:1024, :]
    last = jnp.broadcast_to(legendre_ref[1024:1025, :].astype(F32), (128, 512))
    tail = lax.broadcasted_iota(jnp.int32, (128, 512), 0)
    padded[1024:, :] = jnp.where(tail == 0, last, 0.0).astype(BF16)
    boundary = boundary_ref[0]
    for start in range(0, ROWS, 128):
        odd = 1 if start >= EVEN else 0
        rank = lax.broadcasted_iota(jnp.int32, (128, 1), 0) + (start - odd * EVEN)
        first = (boundary + 1 - odd) >> 1
        source = jnp.where(rank < first, 2 * rank, boundary + 2 * (rank - first)) + odd
        ids = lax.broadcasted_iota(jnp.int32, (128, ROWS), 1)
        pick = jnp.where(ids == source, 1.0, 0.0).astype(BF16)
        rows = dot(pick, padded[...])
        table_ref[start : start + 128, :] = rows.astype(BF16)
        table_t[:, start : start + 128] = rows.T.astype(BF16)
    row = lax.broadcasted_iota(jnp.int32, (144, 72), 0)
    level = lax.broadcasted_iota(jnp.int32, (144, 72), 1)
    pick = jnp.where(level == 9 * ((row >> 1) & 7) + (row >> 4), 1.0, 0.0).astype(BF16)
    row = lax.broadcasted_iota(jnp.int32, (144, 144), 0)
    column = lax.broadcasted_iota(jnp.int32, (144, 144), 1)
    same = (row & 1) == (column & 1)
    for kind in range(2):
        spread = dot(dot(pick, vertical_ref[kind]).astype(BF16), pick, NT)
        mix_ref[kind] = jnp.where(same, spread, 0.0).astype(BF16)


def pair_kernel(
    boundary_ref, data_ref, *refs
):
    hbm, out_ref, held = refs[:7], refs[7], refs[8:15]
    stage_n, stage_s, value_n, value_s, spectral, updated, sems = refs[15:]
    north_ref, south_ref, north_back, south_back, table_ref, table_t, mix_ref = held
    copies = [
        pltpu.make_async_copy(source, target, sems.at[i])
        for i, (source, target) in enumerate(zip(hbm, held))
    ]
    for i in (0, 1, 5, 6, 4, 2, 3):
        copies[i].start()

    def band(half, high, part):
        return ((half * (7 - 2 * high) + high) * 4 + part) * 16

    stages = ((0, stage_n, north_ref, north_back), (1, stage_s, south_ref, south_back))
    for half, stage, _, _ in stages:
        for tile in range(5):
            width = 128 if tile < 4 else 64
            for high in range(4):
                row = (tile * 4 + high) * 32
                for part in range(4):
                    start = band(half, high, part)
                    block = data_ref[start : start + 16, :, tile * 128 : tile * 128 + width]
                    column = part * 128
                    stage[row : row + 32, column : column + width] = block.reshape(32, width)
                    if width == 64:
                        stage[row : row + 32, column + 64 : column + 128] = jnp.zeros((32, 64), BF16)

    pieces = []
    for tile in range(5):
        for group in range(4):
            f, c = tile * 2 + (group >> 1), group & 1
            if f < 9:
                for kind in range(2):
                    pieces.append((tile, group, kind, ((c * 2 + kind) * 9 + f) * 16))

    copies[0].wait()
    copies[1].wait()
    for start in range(0, 640, 128):
        for stage, perm_ref, target in (
            (stage_n, north_ref, value_n), (stage_s, south_ref, value_s)
        ):
            moved = dot(stage[start : start + 128, :], perm_ref[...]).astype(BF16)
            for tile, group, kind, row in pieces:
                if tile * 128 == start:
                    for high in range(4):
                        source = high * 32 + kind * 16
                        target[row : row + 16, high * 128 : high * 128 + 128] = moved[
                            source : source + 16, group * 128 : group * 128 + 128
                        ]

    for i in (5, 6, 4, 2, 3):
        copies[i].wait()
    boundary = boundary_ref[0]
    for odd in range(2):
        low, high = (EVEN, ROWS) if odd else (0, EVEN)
        first = (boundary + 1 - odd) >> 1
        for start in range(low, high, 256):
            size = min(256, high - start)
            rank = lax.broadcasted_iota(jnp.int32, (1, size), 1) + (start - low)
            slots = lax.broadcasted_iota(jnp.int32, (576, size), 0) & 1
            owned = slots == jnp.where(rank < first, 0, 1)
            north = dot(value_n[...], table_t[:, start : start + size])
            south = dot(value_s[...], table_t[:, start : start + size])
            total = north - south if odd else north + south
            spectral[:, start : start + size] = jnp.where(owned, total, 0.0).astype(BF16)
    for block in range(4):
        rows = slice(block * 144, block * 144 + 144)
        updated[rows, :] = dot(mix_ref[block & 1], spectral[rows, :]).astype(BF16)

    for block in range(4):
        rows = slice(block * 144, block * 144 + 144)
        grid_e = dot(updated[rows, :EVEN], table_ref[:EVEN, :])
        grid_o = dot(updated[rows, EVEN:], table_ref[EVEN:, :])
        for stage, grid in ((stage_n, grid_e + grid_o), (stage_s, grid_e - grid_o)):
            grid = grid.astype(BF16)
            for tile, group, kind, row in pieces:
                if row // 144 == block:
                    for high in range(4):
                        target = (tile * 4 + high) * 32 + kind * 16
                        stage[target : target + 16, group * 128 : group * 128 + 128] = grid[
                            row - block * 144 : row - block * 144 + 16, high * 128 : high * 128 + 128
                        ]
    for stage in (stage_n, stage_s):
        stage[512:, 256:] = jnp.zeros((128, 256), BF16)
    for half, stage, _, back_ref in stages:
        for tile in range(5):
            width = 128 if tile < 4 else 64
            moved = dot(stage[tile * 128 : tile * 128 + 128, :], back_ref[...]).astype(BF16)
            for high in range(4):
                for part in range(4):
                    start = band(half, high, part)
                    block = moved[high * 32 : high * 32 + 32, part * 128 : part * 128 + width]
                    out_ref[start : start + 16, :, tile * 128 : tile * 128 + width] = block.reshape(
                        16, 2, width
                    )


VMEM = pl.BlockSpec(memory_space=pltpu.VMEM)
HBM = pl.BlockSpec(memory_space=pltpu.HBM)
SMEM = pl.BlockSpec(memory_space=pltpu.SMEM)
PREPARED = ((512, 512), (512, 512), (512, 512), (512, 512), (ROWS, 512), (512, ROWS), (2, 144, 144))


def prepare(boundary, legendre, vertical):
    return pl.pallas_call(
        prepare_kernel,
        out_shape=[pltpu.HBM(shape, BF16) for shape in PREPARED],
        in_specs=[SMEM, VMEM, VMEM],
        out_specs=[VMEM] * len(PREPARED),
        scratch_shapes=[pltpu.VMEM((ROWS, 512), BF16)],
        compiler_params=pltpu.CompilerParams(vmem_limit_bytes=20 * 1024 * 1024),
        cost_estimate=pl.CostEstimate(
            flops=2_000_000_000, bytes_accessed=6_000_000, transcendentals=0
        ),
    )(boundary, legendre, vertical)


def transform_pair(boundary, data, *prepared):
    return pl.pallas_call(
        pair_kernel,
        out_shape=jax.ShapeDtypeStruct((512, 2, 576), BF16),
        in_specs=[SMEM, VMEM] + [HBM] * len(PREPARED),
        out_specs=VMEM,
        scratch_shapes=[pltpu.VMEM(shape, BF16) for shape in PREPARED]
        + [
            pltpu.VMEM((640, 512), BF16),
            pltpu.VMEM((640, 512), BF16),
            pltpu.VMEM((576, 512), BF16),
            pltpu.VMEM((576, 512), BF16),
            pltpu.VMEM((576, ROWS), BF16),
            pltpu.VMEM((576, ROWS), BF16),
            pltpu.SemaphoreType.DMA((7,)),
        ],
        compiler_params=pltpu.CompilerParams(vmem_limit_bytes=20 * 1024 * 1024),
        cost_estimate=pl.CostEstimate(
            flops=5_000_000_000, bytes_accessed=6_000_000, transcendentals=0
        ),
    )(boundary, data, *(pltpu.with_memory_space_constraint(x, pltpu.HBM) for x in prepared))


def column_of(values, rows):
    count = values.shape[1]
    row = lax.broadcasted_iota(jnp.int32, (16, count), 0)
    digits = jnp.where(row == 0, values >> 5, jnp.where(row == 1, values & 31, 0))
    row = lax.broadcasted_iota(jnp.int32, (rows, count), 0)
    lane = lax.broadcasted_iota(jnp.int32, (rows, count), 1)
    repeat = jnp.where((row >> 1) == lane, 1.0, 0.0).astype(BF16)
    columns = dot(repeat, digits.astype(F32).astype(BF16), NT)
    return columns[:, 0:1] * 32.0 + columns[:, 1:2]


def wave_mask(row_length_ref):
    count = jnp.minimum(1024, row_length_ref[...] >> 1)
    limit = column_of(count, 64).astype(jnp.int32)
    return lax.broadcasted_iota(jnp.int32, (64, 1024), 1) < limit


def order_kernel(
    length_hbm, order_hbm, fourier_hbm, out_hbm, chosen_ref,
    lengths, order, raw, masked, out, in_sems, out_sems,
):
    copies = [
        pltpu.make_async_copy(source, target, in_sems.at[i])
        for i, (source, target) in enumerate(
            ((order_hbm, order), (length_hbm, lengths), (fourier_hbm, raw))
        )
    ]
    for copy in copies:
        copy.start()
    wave_ids = lax.broadcasted_iota(jnp.int32, (256, 1024), 1).astype(jnp.int16)
    odd = (lax.broadcasted_iota(jnp.int32, (256, 1), 0) & 1) == 1
    copies[0].wait()
    for block in range(4):
        wave = column_of(order[:, block * 128 : block * 128 + 128], 256).astype(jnp.int32)
        wave = jnp.where(odd, 1023 - wave, wave).astype(jnp.int16)
        picked = jnp.where(wave_ids == wave, jnp.ones((), BF16), jnp.zeros((), BF16))
        chosen_ref[block * 256 : block * 256 + 256, :] = picked
    copies[1].wait()
    in_range = wave_mask(lengths)
    copies[2].wait()
    for f in range(9):
        kept = jnp.where(in_range, raw[f].reshape(64, 1024), jnp.zeros((), BF16))
        masked[f * 64 : f * 64 + 64, :] = kept
    sent = []
    for block in range(4):
        sorted_rows = dot(chosen_ref[block * 256 : block * 256 + 256, :], masked[...], NT)
        part = slice(block * 128, block * 128 + 128)
        out[part] = sorted_rows.astype(BF16).reshape(128, 2, 576)
        copy = pltpu.make_async_copy(out.at[part], out_hbm.at[part], out_sems.at[block])
        copy.start()
        sent.append(copy)
    for copy in sent:
        copy.wait()


def restore_kernel(length_ref, chosen_ref, data_ref, out_hbm, turned, out, sems):
    in_range = wave_mask(length_ref)
    for block in range(8):
        rows = data_ref[block * 64 : block * 64 + 64].reshape(128, 576)
        turned[:, block * 128 : block * 128 + 128] = rows.T
    sent = []
    for start, size in ((0, 4), (4, 4), (8, 1)):
        restored = dot(turned[start * 64 : (start + size) * 64, :], chosen_ref[...])
        for f in range(size):
            kept = jnp.where(in_range, restored[f * 64 : f * 64 + 64, :], 0.0).astype(BF16)
            out[start + f] = kept.reshape(32, 2, 1024)
        part = slice(start, start + size)
        copy = pltpu.make_async_copy(out.at[part], out_hbm.at[part], sems.at[len(sent)])
        copy.start()
        sent.append(copy)
    for copy in sent:
        copy.wait()


def order_pairs(row_length, wave_order, fourier):
    return pl.pallas_call(
        order_kernel,
        out_shape=(
            pltpu.HBM((512, 2, 576), BF16),
            pltpu.VMEM((1024, 1024), BF16),
        ),
        in_specs=[HBM, HBM, HBM],
        out_specs=(HBM, VMEM),
        scratch_shapes=[
            pltpu.VMEM((1, 32), jnp.int32),
            pltpu.VMEM((1, 512), jnp.int32),
            pltpu.VMEM((9, 32, 2, 1024), BF16),
            pltpu.VMEM((576, 1024), BF16),
            pltpu.VMEM((512, 2, 576), BF16),
            pltpu.SemaphoreType.DMA((3,)),
            pltpu.SemaphoreType.DMA((4,)),
        ],
        compiler_params=pltpu.CompilerParams(vmem_limit_bytes=16 * 1024 * 1024),
    )(*(pltpu.with_memory_space_constraint(x, pltpu.HBM) for x in (row_length, wave_order, fourier)))


def restore_waves(row_length, chosen, data):
    return pl.pallas_call(
        restore_kernel,
        out_shape=jax.ShapeDtypeStruct((9, 32, 2, 1024), BF16),
        in_specs=[VMEM, VMEM, VMEM],
        out_specs=HBM,
        scratch_shapes=[
            pltpu.VMEM((576, 1024), BF16),
            pltpu.VMEM((9, 32, 2, 1024), BF16),
            pltpu.SemaphoreType.DMA((3,)),
        ],
        compiler_params=pltpu.CompilerParams(vmem_limit_bytes=16 * 1024 * 1024),
    )(row_length, chosen, data)


def exchange(chunks):
    return lax.all_to_all(chunks, ("band", "field"), split_axis=0, concat_axis=0, tiled=True)


def per_device(fourier, row_length, wave_order, legendre, vertical):
    position = lax.axis_index("band") * lax.axis_size("field") + lax.axis_index("field")
    lengths = row_length.reshape(1, 32)
    outgoing, chosen = order_pairs(lengths, wave_order.reshape(1, 512), fourier)
    arrived = exchange(outgoing)
    boundary = 1024 - lax.dynamic_slice_in_dim(wave_order, position, 1)
    result = transform_pair(boundary, arrived, *prepare(boundary, legendre[0], vertical))
    return restore_waves(lengths, chosen, exchange(result))


def solution(mesh):
    placed = (P("field", "band", None, None), P("band"), P(), P(("band", "field"), None, None), P())
    return jax.shard_map(
        per_device,
        mesh=mesh,
        in_specs=placed,
        out_specs=P("field", "band", None, None),
        check_vma=False,
    )
```

time: 125 us -> 122 us (0.976)
  matrix products: 1.49 us -> 0 us
  other arithmetic: 1.26 us -> 0 us
    pallas_call x0 -> x1, Pallas kernels: none -> 4.11 us  [prepare(): pl.pallas_call(prepare_kernel, out_shape=[pltpu.HBM(shape, BF16) for shap...]
    pallas_call x1, Pallas kernels: 9.11 us -> 6.4 us  [transform_pair(): pl.pallas_call(pair_kernel, out_shape=jax.ShapeDtypeStruct((512, 2, 576),...]
    pad x1 -> x0, local copies, waits for them, and re-layouts: 2.32 us -> none  [per_device(): table = jnp.pad(legendre[0], ((0, ROWS - 1025), (0, 0)))]
    dot_general x1 -> x0, matrix products: 1.49 us -> none  [dot(): return lax.dot_general(a, b, dims, preferred_element_type=F32)]
  transfers between devices with their start and end apart: 1 -> 1, of which waited for: 1 -> 1; matrix products, arithmetic and copies ran while one was open for 5% -> 1% of each run, Pallas kernels for 0% -> 3%
where the time goes in v2:
time: 122 us
  blocking collectives  47.3 us (39%)
  waiting for transfers between devices  31.8 us (26%)
  starting transfers between devices  22.2 us (18%)
  Pallas kernels  17.4 us (14%)
  local copies, waits for them, and re-layouts  2.5 us (2%)
    all_to_all x1, blocking collectives, exchange(): lax.all_to_all(chunks, ('band', 'field'), split_axis=0, concat_axis=0, ti...  47.3 us
    all_to_all x1, waiting for transfers between devices, exchange(): lax.all_to_all(chunks, ('band', 'field'), split_axis=0, concat_axis=0, ti...  31.8 us
    all_to_all x1, starting transfers between devices, exchange(): lax.all_to_all(chunks, ('band', 'field'), split_axis=0, concat_axis=0, ti...  22.2 us
    pallas_call x1, Pallas kernels, transform_pair(): pl.pallas_call(pair_kernel, out_shape=jax.ShapeDtypeStruct((512, 2, 576),...  6.4 us
    pallas_call x1, Pallas kernels, order_pairs(): pl.pallas_call(order_kernel, out_shape=(pltpu.HBM((512, 2, 576), BF16), p...  4.35 us
    pallas_call x1, Pallas kernels, prepare(): pl.pallas_call(prepare_kernel, out_shape=[pltpu.HBM(shape, BF16) for shap...  4.11 us
    pallas_call x1, Pallas kernels, restore_waves(): pl.pallas_call(restore_kernel, out_shape=jax.ShapeDtypeStruct((9, 32, 2,...  2.55 us
  transfers between devices with their start and end apart: 1, of which 1 were waited for; matrix products, arithmetic and copies ran while one was open for 1% of the time, Pallas kernels for 3%

profile of v2, /device:TPU:1, one launch (start us, length us, event | category | flops | bytes accessed | tf_op | source)
XLA Modules:
  0.0 122.0 jit_solution(345718509144158528)
XLA Ops:
  0.0 4.3 %shard_map.55 = (bf16[512,2,576]{2,1,0:T(2,128)(2,1)}, bf16[1024,1024]{1,0:T(8,128)(2,1)S(1)}) custom-call(s32[1,32]{1,0:T(1,128)} %bitcast.3, s32[1,512]{1,0:T(1,128)} %bitcast.6, bf16[9,32,2,1024]{3,2,1,0:T(2,128)(2,1)} %fourier_hbm.1), custom_call_target="tpu_custom_call" | custom-call | tf_op jit(solution)/shard_map/pallas_call | solution.py:277
  4.4 0.0 copy-start.2
  4.4 22.2 %all-to-all-start = ((bf16[512,2,576]{2,1,0:T(2,128)(2,1)}), bf16[512,2,576]{2,1,0:T(2,128)(2,1)S(1)}, u32[]{:S(2)}, u32[]{:S(2)}) async-start(bf16[512,2,576]{2,1,0:T(2,128)(2,1)} %get-tuple-element.15), calls=%async_computation | async-start | bytes 2621440 | tf_op jit(solution)/shard_map/all_to_all | solution.py:314
  26.6 1.3 %dynamic_slice.3 = s32[1]{0:T(128)} dynamic-slice(s32[512]{0:T(512)} %param.7, s32[]{:T(128)S(6)} %select_n.3), dynamic_slice_sizes={1} | dynamic-slice | bytes 12 | tf_op jit(solution)/shard_map/dynamic_slice | solution.py:322
  28.5 0.0 copy-done.2
  28.5 0.0 copy-start.1
  28.5 1.2 copy-done.1
  29.7 4.1 %shard_map.56 = (bf16[512,512]{1,0:T(8,128)(2,1)}, bf16[512,512]{1,0:T(8,128)(2,1)}, bf16[512,512]{1,0:T(8,128)(2,1)}, bf16[512,512]{1,0:T(8,128)(2,1)}, bf16[11...) custom-call(s32[1]{0:T(128)S(6)} %sub.3.boundary_ref, bf16[1025,512]{1,0:T(8,128)(2,1)S(1)} %bitcast.5, ...), custom_call_target="tpu_custom_call" | custom-call | flops 2000000000 | bytes 6000000 | tf_op jit(solution)/shard_map/pallas_call | solution.py:166
  33.8 31.8 %all-to-all-done.data_ref = bf16[512,2,576]{2,1,0:T(2,128)(2,1)S(1)} async-done(((bf16[512,2,576]{2,1,0:T(2,128)(2,1)}), bf16[512,2,576]{2,1,0:T(2,128)(2,1)S(1)}, u32[]{:S(2)}, u32[]{:S(2)}) %all-to-all-start) | async-done | bytes 1179680 | tf_op jit(solution)/shard_map/all_to_all | solution.py:314
  65.6 6.4 %shard_map.57 = bf16[512,2,576]{2,1,0:T(2,128)(2,1)S(1)} custom-call(s32[1]{0:T(128)S(6)} %sub.3.boundary_ref, bf16[512,2,576]{2,1,0:T(2,128)(2,1)S(1)} %all-to-all-done.data_ref, bf16[512,512]{1,0:T(8,128)(2,1)} %get-tuple-element.16.refs_0_, bf16[512,512]{1,0:T(8,128)(2,1)} %get-tuple-element.17.refs_1_, bf16[512,512]{1,0:T(8,128)(2,1)} %get-tuple-element.18.refs_2_, ...), custom_call_target="tpu_custom_call" | custom-call | flops 5000000000 | bytes 6000000 | tf_op jit(solution)/shard_map/pallas_call | solution.py:180
  72.0 0.0 copy-start
  72.0 47.3 %all_to_all.10.data_ref = bf16[512,2,576]{2,1,0:T(2,128)(2,1)S(1)} all-to-all(bf16[512,2,576]{2,1,0:T(2,128)(2,1)S(1)} %shard_map.57), channel_id=1, replica_groups=mesh['band'=32,'field'=16] {'band','field'}, dimensions={0} | all-to-all | bytes 2359296 | tf_op jit(solution)/shard_map/all_to_all | solution.py:314
  119.3 0.0 copy-done
  119.3 2.5 %shard_map.58 = bf16[9,32,2,1024]{3,2,1,0:T(2,128)(2,1)} custom-call(s32[1,32]{1,0:T(1,128)S(1)} %bitcast.4, bf16[1024,1024]{1,0:T(8,128)(2,1)S(1)} %get-tuple-element.14.chosen_ref, bf16[512,2,576]{2,1,0:T(2,128)(2,1)S(1)} %all_to_all.10.data_ref), custom_call_target="tpu_custom_call" | custom-call | tf_op jit(solution)/shard_map/pallas_call | solution.py:299
Async XLA Ops:
  4.4 24.1 %copy-start.2 = (bf16[2,72,72]{2,1,0:T(8,128)(2,1)S(1)}, bf16[2,72,72]{2,1,0:T(8,128)(2,1)}, u32[]{:S(2)}) copy-start(bf16[2,72,72]{2,1,0:T(8,128)(2,1)} %vertical_ref.1) | copy-start | bytes 62212
  4.4 61.2 %all-to-all-start = ((bf16[512,2,576]{2,1,0:T(2,128)(2,1)}), bf16[512,2,576]{2,1,0:T(2,128)(2,1)S(1)}, u32[]{:S(2)}, u32[]{:S(2)}) async-start(bf16[512,2,576]{2,1,0:T(2,128)(2,1)} %get-tuple-element.15), calls=%async_computation | async-start | bytes 2621440 | tf_op jit(solution)/shard_map/all_to_all | solution.py:314
  28.5 1.2 %copy-start.1 = (bf16[1,1025,512]{2,1,0:T(8,128)(2,1)S(1)}, bf16[1,1025,512]{2,1,0:T(8,128)(2,1)}, u32[]{:S(2)}) copy-start(bf16[1,1025,512]{2,1,0:T(8,128)(2,1)} %param.8) | copy-start | bytes 3148804
  72.0 47.3 %copy-start = (s32[32]{0:T(128)S(1)}, s32[32]{0:T(128)}, u32[]{:S(2)}) copy-start(s32[32]{0:T(128)} %param.6) | copy-start | bytes 388

commit v3 on v2

--- a/solution.py
+++ b/solution.py
@@ -20,16 +20,16 @@
 
 
 def prepare_kernel(
-    boundary_ref, legendre_ref, vertical_ref,
-    north_ref, south_ref, north_back, south_back, table_ref, table_t, mix_ref, padded,
+    boundary_ref, legendre_hbm, north_ref, table_ref, legendre_ref, padded, sem
 ):
+    copy = pltpu.make_async_copy(legendre_hbm, legendre_ref, sem)
+    copy.start()
     row = lax.broadcasted_iota(jnp.int32, (512, 512), 0)
     column = lax.broadcasted_iota(jnp.int32, (512, 512), 1)
-    for a, b, north, south in ((row, column, north_ref, south_ref), (column, row, north_back, south_back)):
-        place = (a >> 7) * 32 + ((a >> 1) & 31)
-        start = ((a >> 6) & 1) * 256 + (a & 1) * 128
-        north[...] = jnp.where(b == start + place, 1.0, 0.0).astype(BF16)
-        south[...] = jnp.where(b == start + 127 - place, 1.0, 0.0).astype(BF16)
+    place = (row >> 7) * 32 + ((row >> 1) & 31)
+    start = ((row >> 6) & 1) * 256 + (row & 1) * 128
+    north_ref[...] = jnp.where(column == start + place, 1.0, 0.0).astype(BF16)
+    copy.wait()
     padded[:1024, :] = legendre_ref[:1024, :]
     last = jnp.broadcast_to(legendre_ref[1024:1025, :].astype(F32), (128, 512))
     tail = lax.broadcasted_iota(jnp.int32, (128, 512), 0)
@@ -42,9 +42,10 @@
         source = jnp.where(rank < first, 2 * rank, boundary + 2 * (rank - first)) + odd
         ids = lax.broadcasted_iota(jnp.int32, (128, ROWS), 1)
         pick = jnp.where(ids == source, 1.0, 0.0).astype(BF16)
-        rows = dot(pick, padded[...])
-        table_ref[start : start + 128, :] = rows.astype(BF16)
-        table_t[:, start : start + 128] = rows.T.astype(BF16)
+        table_ref[start : start + 128, :] = dot(pick, padded[...]).astype(BF16)
+
+
+def mixing(vertical_ref, mix_ref):
     row = lax.broadcasted_iota(jnp.int32, (144, 72), 0)
     level = lax.broadcasted_iota(jnp.int32, (144, 72), 1)
     pick = jnp.where(level == 9 * ((row >> 1) & 7) + (row >> 4), 1.0, 0.0).astype(BF16)
@@ -57,23 +58,22 @@
 
 
 def pair_kernel(
-    boundary_ref, data_ref, *refs
+    boundary_ref, data_ref, vertical_ref, north_ref, table_ref, out_ref,
+    stage_n, stage_s, value_n, value_s, spectral, updated, mix_ref, south_ref,
 ):
-    hbm, out_ref, held = refs[:7], refs[7], refs[8:15]
-    stage_n, stage_s, value_n, value_s, spectral, updated, sems = refs[15:]
-    north_ref, south_ref, north_back, south_back, table_ref, table_t, mix_ref = held
-    copies = [
-        pltpu.make_async_copy(source, target, sems.at[i])
-        for i, (source, target) in enumerate(zip(hbm, held))
-    ]
-    for i in (0, 1, 5, 6, 4, 2, 3):
-        copies[i].start()
+    mixing(vertical_ref, mix_ref)
+    row = lax.broadcasted_iota(jnp.int32, (512, 1), 0)
+    place = (row >> 7) * 32 + ((row >> 1) & 31)
+    goal = ((row >> 6) & 1) * 256 + (row & 1) * 128 + 127 - place
+    column = lax.broadcasted_iota(jnp.int32, (512, 512), 1).astype(jnp.int16)
+    one, nothing = jnp.ones((), BF16), jnp.zeros((), BF16)
+    south_ref[...] = jnp.where(column == goal.astype(jnp.int16), one, nothing)
 
     def band(half, high, part):
         return ((half * (7 - 2 * high) + high) * 4 + part) * 16
 
-    stages = ((0, stage_n, north_ref, north_back), (1, stage_s, south_ref, south_back))
-    for half, stage, _, _ in stages:
+    stages = ((0, stage_n, north_ref), (1, stage_s, south_ref))
+    for half, stage, _ in stages:
         for tile in range(5):
             width = 128 if tile < 4 else 64
             for high in range(4):
@@ -94,8 +94,6 @@
                 for kind in range(2):
                     pieces.append((tile, group, kind, ((c * 2 + kind) * 9 + f) * 16))
 
-    copies[0].wait()
-    copies[1].wait()
     for start in range(0, 640, 128):
         for stage, perm_ref, target in (
             (stage_n, north_ref, value_n), (stage_s, south_ref, value_s)
@@ -109,8 +107,6 @@
                             source : source + 16, group * 128 : group * 128 + 128
                         ]
 
-    for i in (5, 6, 4, 2, 3):
-        copies[i].wait()
     boundary = boundary_ref[0]
     for odd in range(2):
         low, high = (EVEN, ROWS) if odd else (0, EVEN)
@@ -120,8 +116,8 @@
             rank = lax.broadcasted_iota(jnp.int32, (1, size), 1) + (start - low)
             slots = lax.broadcasted_iota(jnp.int32, (576, size), 0) & 1
             owned = slots == jnp.where(rank < first, 0, 1)
-            north = dot(value_n[...], table_t[:, start : start + size])
-            south = dot(value_s[...], table_t[:, start : start + size])
+            north = dot(value_n[...], table_ref[start : start + size, :], NT)
+            south = dot(value_s[...], table_ref[start : start + size, :], NT)
             total = north - south if odd else north + south
             spectral[:, start : start + size] = jnp.where(owned, total, 0.0).astype(BF16)
     for block in range(4):
@@ -143,10 +139,10 @@
                         ]
     for stage in (stage_n, stage_s):
         stage[512:, 256:] = jnp.zeros((128, 256), BF16)
-    for half, stage, _, back_ref in stages:
+    for half, stage, perm_ref in stages:
         for tile in range(5):
             width = 128 if tile < 4 else 64
-            moved = dot(stage[tile * 128 : tile * 128 + 128, :], back_ref[...]).astype(BF16)
+            moved = dot(stage[tile * 128 : tile * 128 + 128, :], perm_ref[...], NT).astype(BF16)
             for high in range(4):
                 for part in range(4):
                     start = band(half, high, part)
@@ -159,44 +155,48 @@
 VMEM = pl.BlockSpec(memory_space=pltpu.VMEM)
 HBM = pl.BlockSpec(memory_space=pltpu.HBM)
 SMEM = pl.BlockSpec(memory_space=pltpu.SMEM)
-PREPARED = ((512, 512), (512, 512), (512, 512), (512, 512), (ROWS, 512), (512, ROWS), (2, 144, 144))
-
-
-def prepare(boundary, legendre, vertical):
+PREPARED = ((512, 512), (ROWS, 512))
+
+
+def prepare(boundary, legendre):
     return pl.pallas_call(
         prepare_kernel,
-        out_shape=[pltpu.HBM(shape, BF16) for shape in PREPARED],
-        in_specs=[SMEM, VMEM, VMEM],
+        out_shape=[pltpu.VMEM(shape, BF16) for shape in PREPARED],
+        in_specs=[SMEM, HBM],
         out_specs=[VMEM] * len(PREPARED),
-        scratch_shapes=[pltpu.VMEM((ROWS, 512), BF16)],
+        scratch_shapes=[
+            pltpu.VMEM((1025, 512), BF16),
+            pltpu.VMEM((ROWS, 512), BF16),
+            pltpu.SemaphoreType.DMA,
+        ],
         compiler_params=pltpu.CompilerParams(vmem_limit_bytes=20 * 1024 * 1024),
         cost_estimate=pl.CostEstimate(
             flops=2_000_000_000, bytes_accessed=6_000_000, transcendentals=0
         ),
-    )(boundary, legendre, vertical)
-
-
-def transform_pair(boundary, data, *prepared):
+    )(boundary, pltpu.with_memory_space_constraint(legendre, pltpu.HBM))
+
+
+def transform_pair(boundary, data, vertical, *prepared):
     return pl.pallas_call(
         pair_kernel,
         out_shape=jax.ShapeDtypeStruct((512, 2, 576), BF16),
-        in_specs=[SMEM, VMEM] + [HBM] * len(PREPARED),
+        in_specs=[SMEM] + [VMEM] * 4,
         out_specs=VMEM,
-        scratch_shapes=[pltpu.VMEM(shape, BF16) for shape in PREPARED]
-        + [
+        scratch_shapes=[
             pltpu.VMEM((640, 512), BF16),
             pltpu.VMEM((640, 512), BF16),
             pltpu.VMEM((576, 512), BF16),
             pltpu.VMEM((576, 512), BF16),
             pltpu.VMEM((576, ROWS), BF16),
             pltpu.VMEM((576, ROWS), BF16),
-            pltpu.SemaphoreType.DMA((7,)),
+            pltpu.VMEM((2, 144, 144), BF16),
+            pltpu.VMEM((512, 512), BF16),
         ],
         compiler_params=pltpu.CompilerParams(vmem_limit_bytes=20 * 1024 * 1024),
         cost_estimate=pl.CostEstimate(
             flops=5_000_000_000, bytes_accessed=6_000_000, transcendentals=0
         ),
-    )(boundary, data, *(pltpu.with_memory_space_constraint(x, pltpu.HBM) for x in prepared))
+    )(boundary, data, vertical, *prepared)
 
 
 def column_of(values, rows):
@@ -217,8 +217,8 @@
 
 
 def order_kernel(
-    length_hbm, order_hbm, fourier_hbm, out_hbm, chosen_ref,
-    lengths, order, raw, masked, out, in_sems, out_sems,
+    length_hbm, order_hbm, fourier_hbm, out_hbm, chosen_hbm,
+    lengths, order, raw, masked, out, chosen_ref, in_sems, out_sems,
 ):
     copies = [
         pltpu.make_async_copy(source, target, in_sems.at[i])
@@ -236,6 +236,8 @@
         wave = jnp.where(odd, 1023 - wave, wave).astype(jnp.int16)
         picked = jnp.where(wave_ids == wave, jnp.ones((), BF16), jnp.zeros((), BF16))
         chosen_ref[block * 256 : block * 256 + 256, :] = picked
+    kept_choice = pltpu.make_async_copy(chosen_ref, chosen_hbm, in_sems.at[3])
+    kept_choice.start()
     copies[1].wait()
     in_range = wave_mask(lengths)
     copies[2].wait()
@@ -252,6 +254,7 @@
         sent.append(copy)
     for copy in sent:
         copy.wait()
+    kept_choice.wait()
 
 
 def restore_kernel(length_ref, chosen_ref, data_ref, out_hbm, turned, out, sems):
@@ -278,17 +281,18 @@
         order_kernel,
         out_shape=(
             pltpu.HBM((512, 2, 576), BF16),
-            pltpu.VMEM((1024, 1024), BF16),
+            pltpu.HBM((1024, 1024), BF16),
         ),
         in_specs=[HBM, HBM, HBM],
-        out_specs=(HBM, VMEM),
+        out_specs=(HBM, HBM),
         scratch_shapes=[
             pltpu.VMEM((1, 32), jnp.int32),
             pltpu.VMEM((1, 512), jnp.int32),
             pltpu.VMEM((9, 32, 2, 1024), BF16),
             pltpu.VMEM((576, 1024), BF16),
             pltpu.VMEM((512, 2, 576), BF16),
-            pltpu.SemaphoreType.DMA((3,)),
+            pltpu.VMEM((1024, 1024), BF16),
+            pltpu.SemaphoreType.DMA((4,)),
             pltpu.SemaphoreType.DMA((4,)),
         ],
         compiler_params=pltpu.CompilerParams(vmem_limit_bytes=16 * 1024 * 1024),
@@ -320,7 +324,7 @@
     outgoing, chosen = order_pairs(lengths, wave_order.reshape(1, 512), fourier)
     arrived = exchange(outgoing)
     boundary = 1024 - lax.dynamic_slice_in_dim(wave_order, position, 1)
-    result = transform_pair(boundary, arrived, *prepare(boundary, legendre[0], vertical))
+    result = transform_pair(boundary, arrived, vertical, *prepare(boundary, legendre[0]))
     return restore_waves(lengths, chosen, exchange(result))
 
 

time: 122 us -> 122 us (level)
  waiting for transfers between devices: 31.8 us -> 34.2 us
  Pallas kernels: 17.4 us -> 16.1 us
    all_to_all x1, waiting for transfers between devices: 31.8 us -> 34.2 us  [exchange(): lax.all_to_all(chunks, ('band', 'field'), split_axis=0, concat_axis=0, ti...]
  transfers between devices with their start and end apart: 1 -> 1, of which waited for: 1 -> 1; matrix products, arithmetic and copies ran while one was open for 1% -> 1% of each run, Pallas kernels for 3% -> 2%
where the time goes in v3:
time: 122 us
  blocking collectives  47.2 us (39%)
  waiting for transfers between devices  34.2 us (28%)
  starting transfers between devices  22.2 us (18%)
  Pallas kernels  16.1 us (13%)
  local copies, waits for them, and re-layouts  1.29 us (1%)
    all_to_all x1, blocking collectives, exchange(): lax.all_to_all(chunks, ('band', 'field'), split_axis=0, concat_axis=0, ti...  47.2 us
    all_to_all x1, waiting for transfers between devices, exchange(): lax.all_to_all(chunks, ('band', 'field'), split_axis=0, concat_axis=0, ti...  34.2 us
    all_to_all x1, starting transfers between devices, exchange(): lax.all_to_all(chunks, ('band', 'field'), split_axis=0, concat_axis=0, ti...  22.2 us
    pallas_call x1, Pallas kernels, transform_pair(): pl.pallas_call(pair_kernel, out_shape=jax.ShapeDtypeStruct((512, 2, 576),...  6.23 us
    pallas_call x1, Pallas kernels, order_pairs(): pl.pallas_call(order_kernel, out_shape=(pltpu.HBM((512, 2, 576), BF16), p...  4.36 us
    pallas_call x1, Pallas kernels, prepare(): pl.pallas_call(prepare_kernel, out_shape=[pltpu.VMEM(shape, BF16) for sha...  2.95 us
    pallas_call x1, Pallas kernels, restore_waves(): pl.pallas_call(restore_kernel, out_shape=jax.ShapeDtypeStruct((9, 32, 2,...  2.55 us
  transfers between devices with their start and end apart: 1, of which 1 were waited for; matrix products, arithmetic and copies ran while one was open for 1% of the time, Pallas kernels for 2%

profile of v3, /device:TPU:1, one launch (start us, length us, event | category | flops | bytes accessed | tf_op | source)
XLA Modules:
  0.0 121.8 jit_solution(8214053015742309448)
XLA Ops:
  0.0 4.4 %shard_map.55 = (bf16[512,2,576]{2,1,0:T(2,128)(2,1)}, bf16[1024,1024]{1,0:T(8,128)(2,1)}) custom-call(s32[1,32]{1,0:T(1,128)} %bitcast.3, s32[1,512]{1,0:T(1,128)} %bitcast.5, bf16[9,32,2,1024]{3,2,1,0:T(2,128)(2,1)} %fourier_hbm.1), custom_call_target="tpu_custom_call" | custom-call | tf_op jit(solution)/shard_map/pallas_call | solution.py:280
  4.4 22.2 %all-to-all-start = ((bf16[512,2,576]{2,1,0:T(2,128)(2,1)}), bf16[512,2,576]{2,1,0:T(2,128)(2,1)S(1)}, u32[]{:S(2)}, u32[]{:S(2)}) async-start(bf16[512,2,576]{2,1,0:T(2,128)(2,1)} %get-tuple-element.10), calls=%async_computation | async-start | bytes 2621440 | tf_op jit(solution)/shard_map/all_to_all | solution.py:318
  26.5 1.3 %dynamic_slice.3 = s32[1]{0:T(128)} dynamic-slice(s32[512]{0:T(512)} %param.7, s32[]{:T(128)S(6)} %select_n.3), dynamic_slice_sizes={1} | dynamic-slice | bytes 12 | tf_op jit(solution)/shard_map/dynamic_slice | solution.py:326
  28.5 0.0 copy-start.2
  28.5 2.9 %shard_map.56 = (bf16[512,512]{1,0:T(8,128)(2,1)S(1)}, bf16[1152,512]{1,0:T(8,128)(2,1)S(1)}) custom-call(s32[1]{0:T(128)S(6)} %sub.3.boundary_ref, bf16[1025,512]{1,0:T(8,128)(2,1)} %bitcast.6), custom_call_target="tpu_custom_call" | custom-call | flops 2000000000 | bytes 6000000 | tf_op jit(solution)/shard_map/pallas_call | solution.py:162
  31.4 34.2 %all-to-all-done.data_ref = bf16[512,2,576]{2,1,0:T(2,128)(2,1)S(1)} async-done(((bf16[512,2,576]{2,1,0:T(2,128)(2,1)}), bf16[512,2,576]{2,1,0:T(2,128)(2,1)S(1)}, u32[]{:S(2)}, u32[]{:S(2)}) %all-to-all-start) | async-done | bytes 1179680 | tf_op jit(solution)/shard_map/all_to_all | solution.py:318
  65.6 0.0 copy-done.2
  65.6 6.2 %shard_map.57 = bf16[512,2,576]{2,1,0:T(2,128)(2,1)S(1)} custom-call(s32[1]{0:T(128)S(6)} %sub.3.boundary_ref, bf16[512,2,576]{2,1,0:T(2,128)(2,1)S(1)} %all-to-all-done.data_ref, bf16[2,72,72]{2,1,0:T(8,128)(2,1)S(1)} %copy-done.2, bf16[512,512]{1,0:T(8,128)(2,1)S(1)} %get-tuple-element.11.north_ref, bf16[1152,512]{1,0:T(8,128)(2,1)S(1)} %get-tuple-element.12.table_ref), custom_call_target="tpu_custom_call" | custom-call | flops 5000000000 | bytes 6000000 | tf_op jit(solution)/shard_map/pallas_call | solution.py:180
  71.8 0.0 copy-start
  71.8 0.0 copy-start.1
  71.8 47.2 %all_to_all.10.data_ref = bf16[512,2,576]{2,1,0:T(2,128)(2,1)S(1)} all-to-all(bf16[512,2,576]{2,1,0:T(2,128)(2,1)S(1)} %shard_map.57), channel_id=1, replica_groups=mesh['band'=32,'field'=16] {'band','field'}, dimensions={0} | all-to-all | bytes 2359296 | tf_op jit(solution)/shard_map/all_to_all | solution.py:318
  119.1 0.0 copy-done
  119.1 0.0 copy-done.1
  119.1 2.6 %shard_map.58 = bf16[9,32,2,1024]{3,2,1,0:T(2,128)(2,1)} custom-call(s32[1,32]{1,0:T(1,128)S(1)} %bitcast.4, bf16[1024,1024]{1,0:T(8,128)(2,1)S(1)} %copy-done, bf16[512,2,576]{2,1,0:T(2,128)(2,1)S(1)} %all_to_all.10.data_ref), custom_call_target="tpu_custom_call" | custom-call | tf_op jit(solution)/shard_map/pallas_call | solution.py:303
Async XLA Ops:
  4.4 61.2 %all-to-all-start = ((bf16[512,2,576]{2,1,0:T(2,128)(2,1)}), bf16[512,2,576]{2,1,0:T(2,128)(2,1)S(1)}, u32[]{:S(2)}, u32[]{:S(2)}) async-start(bf16[512,2,576]{2,1,0:T(2,128)(2,1)} %get-tuple-element.10), calls=%async_computation | async-start | bytes 2621440 | tf_op jit(solution)/shard_map/all_to_all | solution.py:318
  28.5 37.1 %copy-start.2 = (bf16[2,72,72]{2,1,0:T(8,128)(2,1)S(1)}, bf16[2,72,72]{2,1,0:T(8,128)(2,1)}, u32[]{:S(2)}) copy-start(bf16[2,72,72]{2,1,0:T(8,128)(2,1)} %vertical_ref.1) | copy-start | bytes 62212
  71.8 47.3 %copy-start = (bf16[1024,1024]{1,0:T(8,128)(2,1)S(1)}, bf16[1024,1024]{1,0:T(8,128)(2,1)}, u32[]{:S(2)}) copy-start(bf16[1024,1024]{1,0:T(8,128)(2,1)} %get-tuple-element.9.chosen_ref) | copy-start | bytes 6291460
  71.8 47.3 %copy-start.1 = (s32[32]{0:T(128)S(1)}, s32[32]{0:T(128)}, u32[]{:S(2)}) copy-start(s32[32]{0:T(128)} %param.6) | copy-start | bytes 388
